TPU v7x, 128 devices: a whole 4x4x4 slice. The times are simulated.
128 devices in a mesh: req: 16 (over x, z), tp: 8 (over y, core).
Axes of the slice: x: 4, y: 4, z: 4, core: 2. Of those that a mesh axis runs over, the one named last changes fastest.
Arguments:
- tokens: int32 [4, 384], replicated, may hold values from 0 to 32767
- finish: int32 [4, 384], replicated, may hold values from 0 to 1, as said below
- holder: int32 [4, 384], replicated, may hold values from 0 to 15, as said below
- slot_index: int32 [4, 384], replicated, may hold values from 0 to 63, as said below
- embedding: bfloat16 [32768, 8192], P('tp', 'req'), may hold values from -12 to 12, as said below
- norm_gain: float32 [8192], P('req'), may hold values from 0.5 to 1.5
- proj_inner: bfloat16 [8192, 16384], P('req', 'tp'), may hold values from -0.0625 to 0.0625
- proj_gate: bfloat16 [8192, 16384], P('req', 'tp'), may hold values from -0.0625 to 0.0625
- conv_weight: float32 [4, 16384], P(None, 'tp'), may hold values from -2.5 to 2.5
- conv_bias: float32 [16384], P('tp'), may hold values from -2.5 to 2.5
- proj_low: bfloat16 [16384, 512], P('tp'), may hold values from -0.046875 to 0.046875
- proj_select: bfloat16 [32, 16384], P(None, 'tp'), may hold values from -0.046875 to 0.046875
- proj_dt: bfloat16 [512, 16384], P(None, 'tp'), may hold values from -0.25 to 0.25
- dt_bias: float32 [16384], P('tp'), may hold values from -5 to -1.5
- decay_log: float32 [16, 16384], P(None, 'tp'), may hold values from 0 to 2.77
- skip_gain: float32 [16384], P('tp'), may hold values from 0.5 to 1.5
- proj_out: bfloat16 [16384, 8192], P('tp', 'req'), may hold values from -0.046875 to 0.046875
- state_codes: bfloat16 [384, 16, 16384], P('req', None, 'tp'), may hold values from -1 to 1
- state_scales: bfloat16 [384, 128], P('req', 'tp'), may hold values from 0.099609375 to 1
- conv_state: bfloat16 [384, 3, 16384], P('req', None, 'tp'), may hold values from -6 to 6
Outputs:
- mixed: bfloat16 [4, 384, 8192], P(None, None, 'req')
- next_codes: bfloat16 [384, 16, 16384], P('req', None, 'tp')
- next_scales: bfloat16 [384, 128], P('req', 'tp')
- next_window: bfloat16 [384, 3, 16384], P('req', None, 'tp')
- cache_codes: bfloat16 [1024, 16, 16384], P('req', None, 'tp')
- cache_scales: bfloat16 [1024, 128], P('req', 'tp')
- cache_window: bfloat16 [1024, 3, 16384], P('req', None, 'tp')
Inputs may be any that keep to these rules, and one draw needn't show every extreme that they name: `finish`: 1 where the turn ends; in every step, among the rows of one device (aligned blocks of 24 requests), at most 2 finishing requests name the same holder, and this bound is reached. Where finish is 1, the holder of the saved state. Each holder receives at most 64 saves over all steps, and some holder receives exactly 64; other holders may receive far fewer. Where finish is 0 the entry is arbitrary. Where finish is 1, each pair of holder and slot_index occurs at most once over all steps and requests; where finish is 0 the entry is arbitrary. `embedding`: token vectors.
All inputs are finite; a program needn't handle non-finite values.
Results may differ from a plain program's by a relative error of at most 0.035.
Values may be sent and summed in bfloat16 or wider, within the bound.
A program may use at most 128 MiB of HBM per device.

v0:
```python
import jax
import jax.numpy as jnp
from jax import lax
from jax.sharding import PartitionSpec as P

D = 8192
STATE = 16
PAGE = 128
STEPS = 4
CAP = 2


def page_expand(page_values):
    return jnp.repeat(page_values.astype(jnp.float32), PAGE, axis=-1)


def state_update(codes, scales, step_size, activ, b_in, c_out, gate_sum, decay_rate, skip_gain):
    activ_f = activ.astype(jnp.float32)
    previous = codes.astype(jnp.float32) * page_expand(scales)[:, None, :]
    decay = jnp.exp(step_size[:, None, :] * decay_rate[None, :, :])
    current = decay * previous + (step_size * activ_f)[:, None, :] * b_in[:, :, None]
    output = jnp.sum(current * c_out[:, :, None], axis=1) + skip_gain[None, :] * activ_f
    gated = (output * jax.nn.silu(gate_sum)).astype(jnp.bfloat16)
    paged = current.reshape(current.shape[0], current.shape[1], -1, PAGE)
    peak = jnp.max(jnp.abs(paged), axis=(1, 3))
    new_scales = (peak + 1e-06).astype(jnp.bfloat16)
    new_codes = (current / page_expand(new_scales)[:, None, :]).astype(jnp.bfloat16)
    return (gated, new_codes, new_scales)


def block_ranks(flags, owners, rows_each):
    flag_blocks = flags.reshape(-1, rows_each)
    owner_blocks = owners.reshape(-1, rows_each)
    position = jnp.arange(rows_each)
    earlier = position[None, :] < position[:, None]
    ahead = (
        earlier[None]
        & (owner_blocks[:, None, :] == owner_blocks[:, :, None])
        & (flag_blocks[:, None, :] == 1)
    )
    return jnp.sum(ahead.astype(jnp.int32), axis=2).reshape(-1)


def pack_pages(flags, owners, ranks, members, holders):
    target = owners * CAP + ranks
    chosen = (jnp.arange(holders * CAP)[:, None] == target[None, :]) & (flags[None, :] == 1)
    chooser = chosen.astype(jnp.bfloat16)
    packed = []
    for member in members:
        flat = member.reshape(member.shape[0], -1)
        moved = jnp.dot(chooser, flat, preferred_element_type=jnp.float32).astype(jnp.bfloat16)
        packed.append(moved.reshape((holders, CAP) + member.shape[1:]))
    return packed


def place_matrix(flags, owners, places, ranks, self_index, rows_each, holders, slots_dev):
    source_pos = jnp.arange(flags.shape[0]) // rows_each * CAP + ranks
    taken = (flags == 1) & (owners == self_index)
    by_slot = ((places[None, :] == jnp.arange(slots_dev)[:, None]) & taken[None, :]).astype(
        jnp.bfloat16
    )
    by_source = (source_pos[:, None] == jnp.arange(holders * CAP)[None, :]).astype(jnp.bfloat16)
    return jnp.dot(by_slot, by_source, preferred_element_type=jnp.float32)


def store_pages(cache, placement, received):
    written = jnp.sum(placement, axis=1) > 0.5
    chooser = placement.astype(jnp.bfloat16)
    result = []
    for held, arrived in zip(cache, received):
        flat = arrived.reshape(placement.shape[1], -1)
        fresh = jnp.dot(chooser, flat, preferred_element_type=jnp.float32).astype(jnp.bfloat16)
        fresh = fresh.reshape(held.shape)
        result.append(jnp.where(written.reshape((-1,) + (1,) * (held.ndim - 1)), fresh, held))
    return tuple(result)


def per_device(
    tokens,
    finish,
    holder,
    slot_index,
    embedding,
    norm_gain,
    proj_inner,
    proj_gate,
    conv_weight,
    conv_bias,
    proj_low,
    proj_select,
    proj_dt,
    dt_bias,
    decay_log,
    skip_gain,
    proj_out,
    state_codes,
    state_scales,
    conv_state,
):
    holders = lax.axis_size("req")
    self_index = lax.axis_index("req")
    rows_dev = state_codes.shape[0]
    inner_dev = proj_inner.shape[1]
    vocab_dev = embedding.shape[0]
    slots_dev = STEPS * holders * CAP // 2
    local_ids = tokens - lax.axis_index("tp") * vocab_dev
    inside = (local_ids >= 0) & (local_ids < vocab_dev)
    looked = jnp.take(embedding, jnp.clip(local_ids, 0, vocab_dev - 1), axis=0)
    looked = jnp.where(inside[:, :, None], looked, jnp.zeros_like(looked))
    embedded = lax.psum(looked.astype(jnp.float32).astype(jnp.bfloat16), "tp").astype(jnp.float32)
    squares = lax.psum(jnp.sum(embedded * embedded, axis=2), "req")
    inv_rms = lax.rsqrt(squares / D + 1e-05)
    decay_rate = -jnp.exp(decay_log)
    first_row = self_index * rows_dev
    joined = jnp.concatenate([proj_inner, proj_gate], axis=1)
    codes, scales, window = (state_codes, state_scales, conv_state)
    cache = (
        jnp.zeros((slots_dev,) + state_codes.shape[1:], jnp.bfloat16),
        jnp.zeros((slots_dev,) + state_scales.shape[1:], jnp.bfloat16),
        jnp.zeros((slots_dev,) + conv_state.shape[1:], jnp.bfloat16),
    )
    mixed_steps = []
    for step_index in range(STEPS):
        normed = (embedded[step_index] * inv_rms[step_index][:, None] * norm_gain[None, :]).astype(
            jnp.bfloat16
        )
        both_sums = lax.psum_scatter(
            jnp.dot(normed, joined, preferred_element_type=jnp.float32).astype(jnp.bfloat16),
            "req",
            scatter_dimension=0,
            tiled=True,
        ).astype(jnp.float32)
        inner_sum = both_sums[:, :inner_dev]
        gate_sum = both_sums[:, inner_dev:]
        full_window = jnp.concatenate([window, inner_sum.astype(jnp.bfloat16)[:, None, :]], axis=1)
        conv_out = (
            jnp.sum(full_window.astype(jnp.float32) * conv_weight[None], axis=1)
            + conv_bias[None, :]
        )
        activ = jax.nn.silu(conv_out).astype(jnp.bfloat16)
        low_rank, selectors = (
            lax.psum(
                jnp.dot(activ, proj_low, preferred_element_type=jnp.float32).astype(jnp.bfloat16),
                "tp",
            ).astype(jnp.float32),
            lax.psum(
                lax.dot_general(
                    activ, proj_select, (((1,), (1,)), ((), ())), preferred_element_type=jnp.float32
                ).astype(jnp.bfloat16),
                "tp",
            ).astype(jnp.float32),
        )
        step_size = jax.nn.softplus(
            jnp.dot(low_rank.astype(jnp.bfloat16), proj_dt, preferred_element_type=jnp.float32)
            + dt_bias[None, :]
        )
        gated, codes, scales = state_update(
            codes,
            scales,
            step_size,
            activ,
            selectors[:, :STATE],
            selectors[:, STATE:],
            gate_sum,
            decay_rate,
            skip_gain,
        )
        window = full_window[:, 1:]
        projected = jnp.dot(
            lax.all_gather(gated, "req", axis=0, tiled=True),
            proj_out,
            preferred_element_type=jnp.float32,
        )
        mixed_steps.append(lax.psum(projected.astype(jnp.bfloat16), "tp"))
        all_ranks = block_ranks(finish[step_index], holder[step_index], rows_dev)
        own_finish = lax.dynamic_slice_in_dim(finish[step_index], first_row, rows_dev, 0)
        own_holder = lax.dynamic_slice_in_dim(holder[step_index], first_row, rows_dev, 0)
        own_ranks = lax.dynamic_slice_in_dim(all_ranks, first_row, rows_dev, 0)
        send_codes, send_scales, send_window = pack_pages(
            own_finish, own_holder, own_ranks, (codes, scales, window), holders
        )
        placement = place_matrix(
            finish[step_index],
            holder[step_index],
            slot_index[step_index],
            all_ranks,
            self_index,
            rows_dev,
            holders,
            slots_dev,
        )
        received = (
            lax.all_to_all(send_codes, "req", split_axis=0, concat_axis=0, tiled=True),
            lax.all_to_all(send_scales, "req", split_axis=0, concat_axis=0, tiled=True),
            lax.all_to_all(send_window, "req", split_axis=0, concat_axis=0, tiled=True),
        )
        cache = store_pages(cache, placement, received)
    return (jnp.stack(mixed_steps), codes, scales, window, cache[0], cache[1], cache[2])


def solution(mesh):
    in_specs = (
        P(),
        P(),
        P(),
        P(),
        P("tp", "req"),
        P("req"),
        P("req", "tp"),
        P("req", "tp"),
        P(None, "tp"),
        P("tp"),
        P("tp", None),
        P(None, "tp"),
        P(None, "tp"),
        P("tp"),
        P(None, "tp"),
        P("tp"),
        P("tp", "req"),
        P("req", None, "tp"),
        P("req", "tp"),
        P("req", None, "tp"),
    )
    out_specs = (
        P(None, None, "req"),
        P("req", None, "tp"),
        P("req", "tp"),
        P("req", None, "tp"),
        P("req", None, "tp"),
        P("req", "tp"),
        P("req", None, "tp"),
    )
    return jax.shard_map(
        per_device, mesh=mesh, in_specs=in_specs, out_specs=out_specs, check_vma=False
    )
```

profile of v0, /device:TPU:1, one launch (start us, length us, event | category | flops | bytes accessed | tf_op | source)
XLA Modules:
  0.0 806.0 jit_solution(10436287039078948149)
XLA Ops:
  8.1 8.2 %gather_fusion = bf16[1536,512]{1,0:T(8,128)(2,1)} fusion(bf16[4096,512]{1,0:T(8,128)(2,1)} %param.24, s32[2048]{0:T(1024)S(1)} %pad_clamp_fusion), kind=kCustom, calls=%fused_computation | custom fusion | bytes 3151872 | tf_op jit(solution)/shard_map/jit(_take)/gather | solution.py:108
  19.1 3.3 constant_dynamic-update-slice_fusion.1
  23.8 60.6 %all-reduce.12.cloned.1.call-done = bf16[4,384,512]{2,1,0:T(8,128)(2,1)} async-done(((bf16[4,384,512]{2,1,0:T(8,128)(2,1)}), bf16[4,384,512]{2,1,0:T(8,128)(2,1)}) %all-reduce.12.cloned.1.call-update) | async-done | bytes 1572880 | tf_op jit(solution)/shard_map/psum | solution.py:110
  86.2 33.8 %psum.99 = f32[4,384]{1,0:T(4,128)S(1)} all-reduce(f32[4,384]{1,0:T(4,128)S(1)} %multiply_reduce_fusion.4), channel_id=1, replica_groups=mesh['req'=16,'tp'=8] {'req'}, use_global_device_ids=true, to_apply=%region_2.3 | all-reduce | flops 1536 | bytes 12288 | tf_op jit(solution)/shard_map/psum | solution.py:111
  122.0 5.7 convolution_convert_fusion.16
  127.6 5.7 convolution_convert_fusion.17
  133.4 5.7 convolution_convert_fusion.18
  139.1 5.7 convolution_convert_fusion.19
  153.6 174.2 %all-reduce.14.cloned.1.call-done = (bf16[384,4096]{1,0:T(8,128)(2,1)}, bf16[384,4096]{1,0:T(8,128)(2,1)}, bf16[384,4096]{1,0:T(8,128)(2,1)}, bf16[384,4096]{1,0:T(8,128)(2,1)}) async-done(((bf16[384,4096]{1,0:T(8,128)(2,1)}, bf16[384,4096]{1,0:T(8,128)(2,1)}, bf16[384,4096]{1,0:T(8,128)(2,1)}, bf16[384,4096]{1,0:T(8,128)(2,1)}), (bf16[384,4096]{1,0:T(8,128)(2,1)}, bf16[384,4096]{1,0:T(8,128)(2,1)}, ...) | async-done | bytes 12582928
  339.3 55.7 %all-reduce.16.cloned.1.call-done = (bf16[24,32]{1,0:T(8,128)(2,1)}, bf16[24,32]{1,0:T(8,128)(2,1)}, bf16[24,32]{1,0:T(8,128)(2,1)}, bf16[24,32]{1,0:T(8,128)(2,...) async-done(((bf16[24,32]{1,0:T(8,128)(2,1)}, bf16[24,32]{1,0:T(8,128)(2,1)}, ...) | async-done | bytes 104464 | tf_op jit(solution)/shard_map/psum | solution.py:146
  412.2 6.2 multiply_reduce_fusion.2
  421.1 6.2 multiply_reduce_fusion.1
  429.4 6.3 abs_reduce_fusion
  442.4 6.7 all-to-all-start.7
  455.4 5.8 all-to-all-start.6
  462.7 4.8 all-to-all-done.6
  467.6 3.5 all-to-all-start.5
  472.5 4.8 all-to-all-done.5
  477.3 4.4 all-to-all-start.4
  488.3 6.7 all-to-all-start.8
  503.1 5.0 all-to-all-start.9
  513.0 3.2 all-to-all-done.9
  516.1 4.2 all-to-all-start.10
  522.8 5.6 all-to-all-done.10
  528.3 3.6 all-to-all-start.11
  539.8 5.9 all-to-all-start
  551.3 13.0 %all-to-all-done = bf16[16,2,16,2048]{3,2,1,0:T(8,128)(2,1)} async-done(((bf16[16,2,16,2048]{3,2,1,0:T(8,128)(2,1)}), bf16[16,2,16,2048]{3,2,1,0:T(8,128)(2,1)}, u32[]{:S(2)}, u32[]{:S(2)}) %all-to-all-start) | async-done | bytes 2097184 | tf_op jit(solution)/shard_map/all_to_all | solution.py:193
  564.3 7.2 all-to-all-start.1
  578.4 13.5 %all-to-all-done.1 = bf16[16,2,16,2048]{3,2,1,0:T(8,128)(2,1)} async-done(((bf16[16,2,16,2048]{3,2,1,0:T(8,128)(2,1)}), bf16[16,2,16,2048]{3,2,1,0:T(8,128)(2,1)}, u32[]{:S(2)}, u32[]{:S(2)}) %all-to-all-start.1) | async-done | bytes 2097184 | tf_op jit(solution)/shard_map/all_to_all | solution.py:193
  591.9 9.1 %all-to-all-start.2 = ((bf16[16,2,16,2048]{3,2,1,0:T(8,128)(2,1)}), bf16[16,2,16,2048]{3,2,1,0:T(8,128)(2,1)}, u32[]{:S(2)}, u32[]{:S(2)}) async-start(bf16[16,2,16,2048]{3,2,1,0:T(8,128)(2,1)} %bitcast.265), calls=%async_computation.2 | async-start | bytes 4194304 | tf_op jit(solution)/shard_map/all_to_all | solution.py:193
  609.5 9.9 %all-to-all-done.2 = bf16[16,2,16,2048]{3,2,1,0:T(8,128)(2,1)} async-done(((bf16[16,2,16,2048]{3,2,1,0:T(8,128)(2,1)}), bf16[16,2,16,2048]{3,2,1,0:T(8,128)(2,1)}, u32[]{:S(2)}, u32[]{:S(2)}) %all-to-all-start.2) | async-done | bytes 2097184 | tf_op jit(solution)/shard_map/all_to_all | solution.py:193
  619.5 7.3 all-to-all-start.3
  641.8 3.6 reshape.394
  647.7 3.6 reshape.390
  653.2 3.6 reshape.386
  656.8 3.3 select_select_fusion.1
  661.6 4.1 copy.106
  665.6 4.2 copy.110
  669.8 4.1 copy.114
  677.9 4.3 copy.119
  683.6 4.6 copy.115
  689.5 4.4 copy.111
  695.1 4.3 copy.107
  705.7 3.1 fusion.5
  708.9 13.9 %all-gather.7.cloned.1.call-done = bf16[384,2048]{1,0:T(8,128)(2,1)} async-done(((bf16[24,2048]{1,0:T(8,128)(2,1)}), bf16[384,2048]{1,0:T(8,128)(2,1)}) %all-gather.7.cloned.1.call-update) | async-done | bytes 1572880 | tf_op jit(solution)/shard_map/all_gather | solution.py:170
  722.8 3.1 fusion.4
  726.0 8.6 %fusion.2 = bf16[64,16,2048]{2,1,0:T(8,128)(2,1)} fusion(bf16[8,8,16,2048]{3,2,1,0:T(8,128)(2,1)} %copy.119, bf16[8,8,16,2048]{3,2,1,0:T(8,128)(2,1)} %copy.115, bf16[8,8,16,2048]{3,2,1,0:T(8,128)(2,1)} %copy.111, bf16[8,8,16,2048]{3,2,1,0:T(8,128)(2,1)} %copy.107, pred[64]{0:T(512)(128)(4,1)S(1)} %copy-done.72, pred[64]{0:T(512)(128)(4,1)S(1)} %copy-done.74, ...), kind=kLoop, calls=%fused_computation.24 | loop fusion | flops 8388608 | bytes 20971776 | tf_op jit(solution)/shard_map/jit(_where)/select_n | solution.py:74
  734.6 61.6 %all-reduce.18.cloned.1.call-done = (bf16[1,384,512]{2,1,0:T(8,128)(2,1)}, bf16[1,384,512]{2,1,0:T(8,128)(2,1)}, bf16[1,384,512]{2,1,0:T(8,128)(2,1)}, bf16[1,384,512]{2,1,0:T(8,128)(2,1)}) async-done(((bf16[1,384,512]{2,1,0:T(8,128)(2,1)}, bf16[1,384,512]{2,1,0:T(8,128)(2,1)}, bf16[1,384,512]{2,1,0:T(8,128)(2,1)}, bf16[1,384,512]{2,1,0:T(8,128)(2,1)}), (bf16[1,384,512]{2,1,0:T(8,128)(2,1)}, ...) | async-done | bytes 1572880 | tf_op jit(solution)/shard_map/psum | solution.py:174
  (365 shorter events, 153.4 us)
Async XLA Ops:
  7.2 692.3 %copy-start = (bf16[2048,512]{1,0:T(8,128)(2,1)S(1)}, bf16[2048,512]{1,0:T(8,128)(2,1)}, u32[]{:S(2)}) copy-start(bf16[2048,512]{1,0:T(8,128)(2,1)} %param.36) | copy-start | bytes 6291460
  7.2 77.3 %all-reduce.12.cloned.1.call-start = ((), (), s32[]{:S(2)}) async-start(), calls=%async_computation.12 | async-start | bytes 3145728 | tf_op jit(solution)/shard_map/psum | solution.py:110
  19.0 308.7 %all-reduce.14.cloned.1.call-start = ((), (), s32[]{:S(2)}) async-start(), calls=%async_computation.17 | async-start | bytes 25165824
  23.8 98.1 %copy-start.87 = (f32[512]{0:T(512)S(1)}, f32[512]{0:T(512)}, u32[]{:S(2)}) copy-start(f32[512]{0:T(512)} %param.25) | copy-start | bytes 6148
  144.8 185.0 %copy-start.8 = (bf16[24,3,2048]{2,0,1:T(8,128)(2,1)S(1)}, bf16[24,3,2048]{2,0,1:T(8,128)(2,1)}, u32[]{:S(2)}) copy-start(bf16[24,3,2048]{2,0,1:T(8,128)(2,1)} %param.39) | copy-start | bytes 884740
  144.8 185.1 %copy-start.37 = (f32[4,2048]{1,0:T(4,128)S(1)}, f32[4,2048]{1,0:T(4,128)}, u32[]{:S(2)}) copy-start(f32[4,2048]{1,0:T(4,128)} %param.28) | copy-start | bytes 98308
  144.8 185.5 %copy-start.54 = (f32[2048]{0:T(1024)S(1)}, f32[2048]{0:T(1024)}, u32[]{:S(2)}) copy-start(f32[2048]{0:T(1024)} %param.29) | copy-start | bytes 24580
  144.9 250.2 %all-reduce.16.cloned.1.call-start = ((), (), s32[]{:S(2)}) async-start(), calls=%async_computation.18 | async-start | bytes 245760 | tf_op jit(solution)/shard_map/psum | solution.py:146
  149.0 180.9 %copy-start.46 = (s32[384]{0:T(512)}, s32[384]{0:T(512)S(1)}, u32[]{:S(2)}) copy-start(s32[384]{0:T(512)S(1)} %reshape.355) | copy-start | bytes 4612
  149.1 180.8 %copy-start.48 = (s32[384]{0:T(512)}, s32[384]{0:T(512)S(1)}, u32[]{:S(2)}) copy-start(s32[384]{0:T(512)S(1)} %reshape.360) | copy-start | bytes 4612
  149.2 180.7 %copy-start.50 = (s32[384]{0:T(512)}, s32[384]{0:T(512)S(1)}, u32[]{:S(2)}) copy-start(s32[384]{0:T(512)S(1)} %reshape.365) | copy-start | bytes 4612
  149.3 188.5 %copy-start.52 = (s32[384]{0:T(512)}, s32[384]{0:T(512)S(1)}, u32[]{:S(2)}) copy-start(s32[384]{0:T(512)S(1)} %reshape.370) | copy-start | bytes 4612
  334.1 66.2 %copy-start.34 = (f32[2048]{0:T(1024)S(1)}, f32[2048]{0:T(1024)}, u32[]{:S(2)}) copy-start(f32[2048]{0:T(1024)} %param.33) | copy-start | bytes 24580
  337.7 361.8 %all-gather.5.cloned.1.call-start = ((), (), s32[]{:S(2)}) async-start(), calls=%async_computation.13 | async-start | bytes 1671168 | tf_op jit(solution)/shard_map/all_gather | solution.py:170
  398.9 21.6 %copy-start.36 = (f32[24,16]{1,0:T(8,128)}, f32[24,16]{1,0:T(8,128)S(1)}, u32[]{:S(2)}) copy-start(f32[24,16]{1,0:T(8,128)S(1)} %get-tuple-element.107) | copy-start | bytes 4612
  437.9 57.2 %copy-start.30 = (bf16[24,1,2048]{2,0,1:T(8,128)(2,1)S(1)}, bf16[24,1,2048]{2,0,1:T(8,128)(2,1)}, u32[]{:S(2)}) copy-start(bf16[24,1,2048]{2,0,1:T(8,128)(2,1)} %copy-done.29) | copy-start | bytes 294916
  442.4 13.0 %all-to-all-start.7 = ((bf16[16,2,16]{2,1,0:T(2,128)(2,1)}), bf16[16,2,16]{2,1,0:T(2,128)(2,1)}, u32[]{:S(2)}, u32[]{:S(2)}) async-start(bf16[16,2,16]{2,1,0:T(2,128)(2,1)} %bitcast.27), calls=%async_computation.7 | async-start | bytes 16384 | tf_op jit(solution)/shard_map/all_to_all | solution.py:194
  455.4 12.1 %all-to-all-start.6 = ((bf16[16,2,16]{2,1,0:T(2,128)(2,1)}), bf16[16,2,16]{2,1,0:T(2,128)(2,1)S(1)}, u32[]{:S(2)}, u32[]{:S(2)}) async-start(bf16[16,2,16]{2,1,0:T(2,128)(2,1)} %bitcast.25), calls=%async_computation.6 | async-start | bytes 16384 | tf_op jit(solution)/shard_map/all_to_all | solution.py:194
  467.6 33.8 %copy-start.56 = (bf16[16,2,16]{2,1,0:T(2,128)(2,1)}, bf16[16,2,16]{2,1,0:T(2,128)(2,1)S(1)}, u32[]{:S(2)}) copy-start(bf16[16,2,16]{2,1,0:T(2,128)(2,1)S(1)} %all-to-all-done.6) | copy-start | bytes 3076
  467.6 9.8 %all-to-all-start.5 = ((bf16[16,2,16]{2,1,0:T(2,128)(2,1)}), bf16[16,2,16]{2,1,0:T(2,128)(2,1)S(1)}, u32[]{:S(2)}, u32[]{:S(2)}) async-start(bf16[16,2,16]{2,1,0:T(2,128)(2,1)} %bitcast.23), calls=%async_computation.5 | async-start | bytes 16384 | tf_op jit(solution)/shard_map/all_to_all | solution.py:194
  477.3 11.0 %all-to-all-start.4 = ((bf16[16,2,16]{2,1,0:T(2,128)(2,1)}), bf16[16,2,16]{2,1,0:T(2,128)(2,1)}, u32[]{:S(2)}, u32[]{:S(2)}) async-start(bf16[16,2,16]{2,1,0:T(2,128)(2,1)} %bitcast.21), calls=%async_computation.4 | async-start | bytes 16384 | tf_op jit(solution)/shard_map/all_to_all | solution.py:194
  488.3 14.8 %all-to-all-start.8 = ((bf16[16,2,3,2048]{3,1,2,0:T(2,128)(2,1)}), bf16[16,2,3,2048]{3,1,2,0:T(2,128)(2,1)}, u32[]{:S(2)}, u32[]{:S(2)}) async-start(bf16[16,2,3,2048]{3,1,2,0:T(2,128)(2,1)} %copy.78), calls=%async_computation.8 | async-start | bytes 786432 | tf_op jit(solution)/shard_map/all_to_all | solution.py:195
  499.1 21.3 %copy-start.27 = (bf16[24,1,2048]{2,0,1:T(8,128)(2,1)S(1)}, bf16[24,1,2048]{2,0,1:T(8,128)(2,1)}, u32[]{:S(2)}) copy-start(bf16[24,1,2048]{2,0,1:T(8,128)(2,1)} %copy-done.26) | copy-start | bytes 294916
  503.1 13.0 %all-to-all-start.9 = ((bf16[16,2,3,2048]{3,1,2,0:T(2,128)(2,1)}), bf16[16,2,3,2048]{3,1,2,0:T(2,128)(2,1)}, u32[]{:S(2)}, u32[]{:S(2)}) async-start(bf16[16,2,3,2048]{3,1,2,0:T(2,128)(2,1)} %copy.81), calls=%async_computation.9 | async-start | bytes 786432 | tf_op jit(solution)/shard_map/all_to_all | solution.py:195
  516.1 12.2 %all-to-all-start.10 = ((bf16[16,2,3,2048]{3,1,2,0:T(2,128)(2,1)}), bf16[16,2,3,2048]{3,1,2,0:T(2,128)(2,1)}, u32[]{:S(2)}, u32[]{:S(2)}) async-start(bf16[16,2,3,2048]{3,1,2,0:T(2,128)(2,1)} %copy.84), calls=%async_computation.10 | async-start | bytes 786432 | tf_op jit(solution)/shard_map/all_to_all | solution.py:195
  520.4 182.2 %all-gather.11.cloned.1.call-start = ((), (), s32[]{:S(2)}) async-start(), calls=%async_computation.16 | async-start | bytes 1671168 | tf_op jit(solution)/shard_map/all_gather | solution.py:170
  528.3 11.5 %all-to-all-start.11 = ((bf16[16,2,3,2048]{3,1,2,0:T(2,128)(2,1)}), bf16[16,2,3,2048]{3,1,2,0:T(2,128)(2,1)S(1)}, u32[]{:S(2)}, u32[]{:S(2)}) async-start(bf16[16,2,3,2048]{3,1,2,0:T(2,128)(2,1)} %copy.87), calls=%async_computation.11 | async-start | bytes 786432 | tf_op jit(solution)/shard_map/all_to_all | solution.py:195
  539.8 24.5 %all-to-all-start = ((bf16[16,2,16,2048]{3,2,1,0:T(8,128)(2,1)}), bf16[16,2,16,2048]{3,2,1,0:T(8,128)(2,1)}, u32[]{:S(2)}, u32[]{:S(2)}) async-start(bf16[16,2,16,2048]{3,2,1,0:T(8,128)(2,1)} %bitcast.269), calls=%async_computation | async-start | bytes 4194304 | tf_op jit(solution)/shard_map/all_to_all | solution.py:193
  551.2 20.9 %copy-start.51 = (s32[384]{0:T(512)S(1)}, s32[384]{0:T(512)}, u32[]{:S(2)}) copy-start(s32[384]{0:T(512)} %copy-done.50) | copy-start | bytes 4612
  551.2 20.9 %copy-start.81 = (s32[384]{0:T(512)S(1)}, s32[384]{0:T(512)}, u32[]{:S(2)}) copy-start(s32[384]{0:T(512)} %get-tuple-element.51) | copy-start | bytes 4612
  551.2 20.9 %copy-start.85 = (pred[384]{0:T(512)(128)(4,1)S(1)}, pred[384]{0:T(512)(128)(4,1)}, u32[]{:S(2)}) copy-start(pred[384]{0:T(512)(128)(4,1)} %get-tuple-element.42) | copy-start | bytes 1156
  551.2 21.3 %copy-start.80 = (s32[384]{0:T(512)S(1)}, s32[384]{0:T(512)}, u32[]{:S(2)}) copy-start(s32[384]{0:T(512)} %get-tuple-element.49) | copy-start | bytes 4612
  551.3 21.3 %copy-start.84 = (pred[384]{0:T(512)(128)(4,1)S(1)}, pred[384]{0:T(512)(128)(4,1)}, u32[]{:S(2)}) copy-start(pred[384]{0:T(512)(128)(4,1)} %get-tuple-element.41) | copy-start | bytes 1156
  564.3 27.6 %all-to-all-start.1 = ((bf16[16,2,16,2048]{3,2,1,0:T(8,128)(2,1)}), bf16[16,2,16,2048]{3,2,1,0:T(8,128)(2,1)}, u32[]{:S(2)}, u32[]{:S(2)}) async-start(bf16[16,2,16,2048]{3,2,1,0:T(8,128)(2,1)} %bitcast.266), calls=%async_computation.1 | async-start | bytes 4194304 | tf_op jit(solution)/shard_map/all_to_all | solution.py:193
  571.5 134.2 %all-gather.9.cloned.1.call-start = ((), (), s32[]{:S(2)}) async-start(), calls=%async_computation.15 | async-start | bytes 1671168 | tf_op jit(solution)/shard_map/all_gather | solution.py:170
  572.1 36.3 %copy-start.71 = (pred[64]{0:T(512)(128)(4,1)}, pred[64]{0:T(512)(128)(4,1)S(1)}, u32[]{:S(2)}) copy-start(pred[64]{0:T(512)(128)(4,1)S(1)} %broadcast_compare_fusion) | copy-start | bytes 196
  572.8 54.2 %copy-start.38 = (bf16[64,32]{0,1:T(8,128)(2,1)}, bf16[64,32]{0,1:T(8,128)(2,1)S(1)}, u32[]{:S(2)}) copy-start(bf16[64,32]{0,1:T(8,128)(2,1)S(1)} %get-tuple-element.123) | copy-start | bytes 12292
  578.4 22.7 %copy-start.47 = (s32[384]{0:T(512)S(1)}, s32[384]{0:T(512)}, u32[]{:S(2)}) copy-start(s32[384]{0:T(512)} %copy-done.46) | copy-start | bytes 4612
  578.4 22.7 %copy-start.79 = (s32[384]{0:T(512)S(1)}, s32[384]{0:T(512)}, u32[]{:S(2)}) copy-start(s32[384]{0:T(512)} %get-tuple-element.48) | copy-start | bytes 4612
  578.4 22.7 %copy-start.83 = (pred[384]{0:T(512)(128)(4,1)S(1)}, pred[384]{0:T(512)(128)(4,1)}, u32[]{:S(2)}) copy-start(pred[384]{0:T(512)(128)(4,1)} %get-tuple-element.40) | copy-start | bytes 1156
  578.4 23.1 %copy-start.25 = (bf16[24,1,2048]{2,0,1:T(8,128)(2,1)S(1)}, bf16[24,1,2048]{2,0,1:T(8,128)(2,1)}, u32[]{:S(2)}) copy-start(bf16[24,1,2048]{2,0,1:T(8,128)(2,1)} %copy-done.24) | copy-start | bytes 294916
  591.9 27.6 %all-to-all-start.2 = ((bf16[16,2,16,2048]{3,2,1,0:T(8,128)(2,1)}), bf16[16,2,16,2048]{3,2,1,0:T(8,128)(2,1)}, u32[]{:S(2)}, u32[]{:S(2)}) async-start(bf16[16,2,16,2048]{3,2,1,0:T(8,128)(2,1)} %bitcast.265), calls=%async_computation.2 | async-start | bytes 4194304 | tf_op jit(solution)/shard_map/all_to_all | solution.py:193
  601.0 121.8 %all-gather.7.cloned.1.call-start = ((), (), s32[]{:S(2)}) async-start(), calls=%async_computation.14 | async-start | bytes 1671168 | tf_op jit(solution)/shard_map/all_gather | solution.py:170
  601.1 25.9 %copy-start.75 = (pred[64]{0:T(512)(128)(4,1)}, pred[64]{0:T(512)(128)(4,1)S(1)}, u32[]{:S(2)}) copy-start(pred[64]{0:T(512)(128)(4,1)S(1)} %broadcast_compare_fusion.2) | copy-start | bytes 196
  601.5 25.8 %copy-start.40 = (bf16[64,32]{0,1:T(8,128)(2,1)}, bf16[64,32]{0,1:T(8,128)(2,1)S(1)}, u32[]{:S(2)}) copy-start(bf16[64,32]{0,1:T(8,128)(2,1)S(1)} %get-tuple-element.125) | copy-start | bytes 12292
  601.5 25.7 %copy-start.77 = (pred[64]{0:T(512)(128)(4,1)}, pred[64]{0:T(512)(128)(4,1)S(1)}, u32[]{:S(2)}) copy-start(pred[64]{0:T(512)(128)(4,1)S(1)} %broadcast_compare_fusion.3) | copy-start | bytes 196
  619.5 54.4 %all-to-all-start.3 = ((bf16[16,2,16,2048]{3,2,1,0:T(8,128)(2,1)}), bf16[16,2,16,2048]{3,2,1,0:T(8,128)(2,1)}, u32[]{:S(2)}, u32[]{:S(2)}) async-start(bf16[16,2,16,2048]{3,2,1,0:T(8,128)(2,1)} %bitcast.264), calls=%async_computation.3 | async-start | bytes 4194304 | tf_op jit(solution)/shard_map/all_to_all | solution.py:193
  626.8 169.5 %all-reduce.18.cloned.1.call-start = ((), (), s32[]{:S(2)}) async-start(), calls=%async_computation.19 | async-start | bytes 3145728 | tf_op jit(solution)/shard_map/psum | solution.py:174
  (61 other events, 485.0 us)
Sparse Core Ops, SparseCore 0:
  19.1 65.2 all-reduce.11
  145.0 182.7 all-reduce.13
  337.8 57.1 all-reduce.15
  438.1 44.2 all-gather.4
  523.1 71.4 all-gather.10
  596.6 66.0 all-gather.8
  664.9 57.9 all-gather.6
  726.1 70.0 all-reduce.17
where the time goes:
time: 817 us; the launch traced here: 806 us
  waiting for transfers between devices  425 us (52%)
  local copies, waits for them, and re-layouts  121 us (15%)
  matrix products  77.4 us (9%)
  starting transfers between devices  70.1 us (9%)
  other arithmetic  62.5 us (8%)
  blocking collectives  33.8 us (4%)
  between operations  16.6 us (2%)
    unnamed x9, waiting for transfers between devices  174 us
    unnamed x211, local copies, waits for them, and re-layouts  66 us
    psum x1, waiting for transfers between devices, per_device(): mixed_steps.append(lax.psum(projected.astype(jnp.bfloat16), 'tp'))  61.6 us
    psum x1, waiting for transfers between devices, per_device(): lax.psum(looked.astype(jnp.float32).astype(jnp.bfloat16), 'tp')  60.6 us
    psum x1, waiting for transfers between devices, per_device(): lax.psum(lax.dot_general(activ, proj_select, (((1,), (1,)), ((), ())), pr...  55.7 us
    all_to_all x4, waiting for transfers between devices, per_device(): lax.all_to_all(send_codes, 'req', split_axis=0, concat_axis=0, tiled=True)  36.5 us
    psum x1, blocking collectives, per_device(): squares = lax.psum(jnp.sum(embedded * embedded, axis=2), 'req')  33.8 us
    all_to_all x4, starting transfers between devices, per_device(): lax.all_to_all(send_codes, 'req', split_axis=0, concat_axis=0, tiled=True)  29.4 us
  transfers between devices with their start and end apart: 20, of which 15 were waited for; matrix products, arithmetic and copies ran while one was open for 20% of the time, Pallas kernels for 0%

commit v1 on v0

v1 whole, which is shorter than its diff:
```python
import functools

import jax
import jax.numpy as jnp
from jax import lax
from jax.experimental import pallas as pl
from jax.experimental.pallas import tpu as pltpu
from jax.sharding import PartitionSpec as P

D = 8192
STATE = 16
PAGE = 128
STEPS = 4
CAP = 2
ROWS = 24
BLOCKS = 16
BROWS = STEPS * ROWS
SLOTS = 64
INNER = 2048
FEATS = 512
WIDE = 512
RANK = 512
PAIRS = STEPS * CAP
F32 = jnp.float32
BF16 = jnp.bfloat16
MESH = pl.DeviceIdType.MESH
VMEM_LIMIT = 60 * 1024 * 1024


def rcopy(src, dst, send, recv, dev):
    return pltpu.make_async_remote_copy(
        src_ref=src, dst_ref=dst, send_sem=send, recv_sem=recv, device_id=dev, device_id_type=MESH
    )


def mod4(v):
    return lax.rem(v + 8, 4)


def dot(a, b):
    return jnp.dot(a, b, preferred_element_type=F32)


def greet(devices):
    barrier = pltpu.get_barrier_semaphore()
    for dev in devices:
        pl.semaphore_signal(barrier, inc=1, device_id=dev, device_id_type=MESH)
    pl.semaphore_wait(barrier, len(devices))


TP_SCRATCH = [
    pltpu.VMEM((4, 2, BROWS, FEATS), BF16),
    pltpu.VMEM((4, 2, BROWS, FEATS), BF16),
    pltpu.VMEM((4, 2, BROWS, FEATS), F32),
    pltpu.VMEM((2, BROWS, FEATS), BF16),
    pltpu.VMEM((2, BROWS, FEATS), BF16),
    pltpu.VMEM((2, BROWS, FEATS), BF16),
    pltpu.VMEM((2, BROWS, FEATS), BF16),
    pltpu.VMEM((2, BROWS, FEATS), BF16),
    pltpu.VMEM((2, BROWS, FEATS), BF16),
    pltpu.SemaphoreType.DMA((20,)),
    pltpu.SemaphoreType.DMA((20,)),
]


def tp_partners():
    r, t = lax.axis_index("req"), lax.axis_index("tp")
    y, c = lax.div(t, 2), lax.rem(t, 2)
    return [(r, y * 2 + 1 - c), (r, mod4(y + 1) * 2 + c), (r, mod4(y - 1) * 2 + c)]


def tp_sum(get, total, bufs):
    half_s, half_r, part, far_s, far_r, dir_s, dir_r, com_s, com_r, ss, rs = bufs
    t = lax.axis_index("tp")
    y, c = lax.div(t, 2), lax.rem(t, 2)
    core, up, down = tp_partners()
    order = [mod4(y + 2), mod4(y + 1), mod4(y - 1), y]
    sent = []

    def send(src, dst, n, dev):
        copy = rcopy(src, dst, ss.at[n], rs.at[n], dev)
        copy.start()
        sent.append(copy)

    def arrived(ref, n):
        rcopy(ref, ref, ss.at[n], rs.at[n], core).wait_recv()

    def pair(group, yy):
        return pl.ds(2 * (group * 4 + yy), 2)

    for k in range(4):
        half_s[k] = get((1 - c) * 4 + order[k]).astype(BF16)
        send(half_s.at[k], half_r.at[k], k, core)
    for k in range(4):
        mine = get(c * 4 + order[k])
        arrived(half_r.at[k], k)
        part[k] = mine + half_r[k].astype(F32)
        if k == 0:
            far_s[...] = part[0].astype(BF16)
            send(far_s.at[0], far_r.at[0], 4, up)
            send(far_s.at[1], far_r.at[1], 5, down)
        if k == 1:
            dir_s[1] = part[1, 1].astype(BF16)
            send(dir_s.at[1], dir_r.at[1], 7, up)
        if k == 2:
            dir_s[0] = part[2, 0].astype(BF16)
            send(dir_s.at[0], dir_r.at[0], 6, down)
    arrived(far_r.at[0], 4)
    com_s[0] = (part[1, 0] + far_r[0].astype(F32)).astype(BF16)
    send(com_s.at[0], com_r.at[0], 8, up)
    arrived(far_r.at[1], 5)
    com_s[1] = (part[2, 1] + far_r[1].astype(F32)).astype(BF16)
    send(com_s.at[1], com_r.at[1], 9, down)
    own = 2 * (c * 4 + y)
    for h in range(2):
        arrived(dir_r.at[h], 6 + h)
        arrived(com_r.at[h], 8 + h)
        total[own + h] = (part[3, h] + dir_r[h].astype(F32) + com_r[h].astype(F32)).astype(BF16)
    mine = total.at[pair(c, y)]
    send(mine, mine, 10, up)
    send(mine, mine, 11, down)
    send(mine, mine, 12, core)
    below = total.at[pair(c, mod4(y - 1))]
    above = total.at[pair(c, mod4(y + 1))]
    arrived(below, 10)
    first = total.at[2 * (c * 4 + mod4(y - 1))]
    send(first, first, 13, up)
    send(below, below, 15, core)
    arrived(above, 11)
    second = total.at[2 * (c * 4 + mod4(y + 1)) + 1]
    send(second, second, 14, down)
    send(above, above, 16, core)
    far = 2 * (c * 4 + mod4(y + 2))
    arrived(total.at[far], 13)
    send(total.at[far], total.at[far], 17, core)
    arrived(total.at[far + 1], 14)
    send(total.at[far + 1], total.at[far + 1], 18, core)
    arrived(total.at[pair(1 - c, y)], 12)
    arrived(total.at[pair(1 - c, mod4(y - 1))], 15)
    arrived(total.at[pair(1 - c, mod4(y + 1))], 16)
    other = 2 * ((1 - c) * 4 + mod4(y + 2))
    arrived(total.at[other], 17)
    arrived(total.at[other + 1], 18)
    for copy in sent:
        copy.wait_send()


def shift_req(axis, d):
    r, t = lax.axis_index("req"), lax.axis_index("tp")
    x, z = lax.div(r, 4), lax.rem(r, 4)
    if axis == 0:
        return (mod4(x + d) * 4 + z, t)
    return (x * 4 + mod4(z + d), t)


def req_place(axis):
    r = lax.axis_index("req")
    return lax.div(r, 4) if axis == 0 else lax.rem(r, 4)


def req_partners():
    return [shift_req(axis, d) for axis in (0, 1) for d in (1, -1)]


FRONT_SCRATCH = (
    [
        pltpu.VMEM((BLOCKS, BROWS, FEATS), BF16),
        pltpu.VMEM((4, 4 * BROWS, FEATS), BF16),
        pltpu.VMEM((4, 4 * BROWS, FEATS), BF16),
        pltpu.VMEM((4, 4 * BROWS, PAGE), F32),
    ]
    + [pltpu.VMEM((2, 4, 4 * BROWS, WIDE), BF16)] * 6
    + [pltpu.VMEM((2, 4, BROWS, WIDE), BF16)] * 6
    + [pltpu.VMEM((2, 4, 4, BROWS, WIDE), F32)]
    + [pltpu.SemaphoreType.DMA((6, 2, 4)), pltpu.SemaphoreType.DMA((6, 2, 4))]
    + [pltpu.VMEM((4 * BROWS, PAGE), BF16)] * 6
    + [pltpu.VMEM((BROWS, PAGE), BF16)] * 6
    + [pltpu.VMEM((4, BROWS, PAGE), F32)]
    + [pltpu.SemaphoreType.DMA((6,)), pltpu.SemaphoreType.DMA((6,))]
)


class ScatterSum:
    def __init__(self, axis, d, partial, bufs, total, ss, rs):
        self.axes = (axis, 1 - axis)
        self.d = d
        self.partial = partial
        self.far_s, self.far_r, self.dir_s, self.dir_r, self.com_s, self.com_r = bufs[:6]
        self.far2_s, self.far2_r, self.dir2_s, self.dir2_r, self.com2_s, self.com2_r = bufs[6:]
        self.total = total
        self.ss, self.rs = ss, rs

    def copy(self, n):
        src = (self.far_s, self.dir_s, self.com_s, self.far2_s, self.dir2_s, self.com2_s)[n]
        dst = (self.far_r, self.dir_r, self.com_r, self.far2_r, self.dir2_r, self.com2_r)[n]
        d = -self.d if n % 3 == 1 else self.d
        return rcopy(src, dst, self.ss(n), self.rs(n), shift_req(self.axes[n // 3], d))

    def far(self):
        p = req_place(self.axes[0])
        self.far_s[...] = self.partial(mod4(p + 2)).astype(BF16)
        self.copy(0).start()

    def direct(self):
        p = req_place(self.axes[0])
        self.dir_s[...] = self.partial(mod4(p - self.d)).astype(BF16)
        self.copy(1).start()

    def combined(self):
        p = req_place(self.axes[0])
        mine = self.partial(mod4(p + self.d))
        self.copy(0).wait_recv()
        self.com_s[...] = (mine + self.far_r[...].astype(F32)).astype(BF16)
        self.copy(2).start()

    def own(self):
        p, q = req_place(self.axes[0]), req_place(self.axes[1])
        mine = self.partial(p)
        self.copy(1).wait_recv()
        self.copy(2).wait_recv()
        mine = mine + self.dir_r[...].astype(F32) + self.com_r[...].astype(F32)
        self.total[...] = mine.reshape(4, BROWS, mine.shape[1])
        self.far2_s[...] = self.total[mod4(q + 2)].astype(BF16)
        self.copy(3).start()
        self.dir2_s[...] = self.total[mod4(q - self.d)].astype(BF16)
        self.copy(4).start()

    def combined2(self):
        q = req_place(self.axes[1])
        self.copy(3).wait_recv()
        self.com2_s[...] = (self.total[mod4(q + self.d)] + self.far2_r[...].astype(F32)).astype(
            BF16
        )
        self.copy(5).start()

    def result(self):
        q = req_place(self.axes[1])
        self.copy(4).wait_recv()
        self.copy(5).wait_recv()
        return self.total[q] + self.dir2_r[...].astype(F32) + self.com2_r[...].astype(F32)

    def drain(self):
        for n in range(6):
            self.copy(n).wait_send()


def front_kernel(ids, emb, gain, w_inner, w_gate, out, *scratch):
    tp_bufs, rest = scratch[: len(TP_SCRATCH)], scratch[len(TP_SCRATCH) :]
    embedded, lhs_x, lhs_z, squares = rest[:4]
    big = rest[4:17]
    big_ss, big_rs = rest[17:19]
    small = rest[19:32]
    small_ss, small_rs = rest[32:34]
    greet(tp_partners() + req_partners())

    def looked(ch):
        want = ids[pl.ds(2 * ch, 2)].reshape(2 * BROWS, 1)
        span = 1024
        acc = jnp.zeros((2 * BROWS, FEATS), F32)
        for k in range(emb.shape[0] // span):
            lane = lax.broadcasted_iota(jnp.int32, (2 * BROWS, span), 1) + k * span
            hot = jnp.where(lane == want, 1.0, 0.0).astype(BF16)
            acc = acc + dot(hot, emb[k * span : (k + 1) * span, :])
        return acc.reshape(2, BROWS, FEATS)

    tp_sum(looked, embedded, tp_bufs)

    def spread(b, carry):
        x, z = lax.div(b, 4), lax.rem(b, 4)
        rows = embedded[b].astype(F32)
        scaled = (rows * gain[...]).astype(BF16)
        lhs_x[x, pl.ds(pl.multiple_of(z * BROWS, BROWS), BROWS), :] = scaled
        lhs_z[z, pl.ds(pl.multiple_of(x * BROWS, BROWS), BROWS), :] = scaled
        squares[x, pl.ds(pl.multiple_of(z * BROWS, BROWS), BROWS), :] = jnp.broadcast_to(
            jnp.sum(rows * rows, axis=1, keepdims=True), (BROWS, PAGE)
        )
        return carry

    lax.fori_loop(0, BLOCKS, spread, 0)

    def unit(ab, u):
        lhs, weight = ((lhs_x, w_inner), (lhs_z, w_gate))[ab]

        def partial(chunk):
            cols = pl.ds(pl.multiple_of(u * WIDE, WIDE), WIDE)
            return dot(lhs[chunk], weight[:, cols])

        views = [ref.at[ab, u] for ref in big[:12]]
        return ScatterSum(
            ab,
            1 - 2 * lax.rem(u, 2),
            partial,
            views,
            big[12].at[ab, u],
            lambda n: big_ss.at[n, ab, u],
            lambda n: big_rs.at[n, ab, u],
        )

    norm = ScatterSum(
        0, 1, lambda chunk: squares[chunk], small[:12], small[12],
        lambda n: small_ss.at[n], lambda n: small_rs.at[n],
    )

    def each(step):
        def body(u, carry):
            for ab in range(2):
                step(ab, u, unit(ab, u))
            return carry

        lax.fori_loop(0, 4, body, 0)

    norm.far()
    each(lambda ab, u, s: s.far())
    norm.direct()
    each(lambda ab, u, s: s.direct())
    norm.combined()
    each(lambda ab, u, s: s.combined())
    norm.own()
    each(lambda ab, u, s: s.own())
    norm.combined2()
    each(lambda ab, u, s: s.combined2())
    inv_rms = lax.rsqrt(norm.result()[:, :1] / D + 1e-05)

    def finish(ab, u, s):
        cols = pl.ds(pl.multiple_of((ab * 4 + u) * WIDE, WIDE), WIDE)
        out[:, cols] = s.result() * inv_rms

    each(finish)
    norm.drain()
    each(lambda ab, u, s: s.drain())


def vmem_call(kernel, out_shape, n_in, scratch, **params):
    spec = pl.BlockSpec(memory_space=pltpu.VMEM)
    return pl.pallas_call(
        kernel,
        out_shape=out_shape,
        in_specs=[spec] * n_in,
        out_specs=jax.tree.map(lambda _: spec, out_shape),
        scratch_shapes=scratch,
        compiler_params=pltpu.CompilerParams(vmem_limit_bytes=VMEM_LIMIT, **params),
    )


def silu(v):
    return v / (1.0 + jnp.exp(-v))


RCOLS = RANK + 128


def rank_kernel(
    sums, conv, taps, bias, w_low, w_select, w_dt, dt_bias, step, activ, select,
    pair_s, pair_r, quad_s, quad_r, full, ss, rs,
):
    r, t = lax.axis_index("req"), lax.axis_index("tp")
    y, c = lax.div(t, 2), lax.rem(t, 2)
    core = (r, y * 2 + 1 - c)
    others = [(r, mod4(y + d) * 2 + c) for d in (1, 2, 3)]
    greet([core] + others)
    for n in range(STEPS):
        total = bias[...] + jnp.zeros((ROWS, INNER), F32)
        for k in range(4):
            at = n + k
            if at < 3:
                row = conv[at * ROWS : (at + 1) * ROWS, :]
            else:
                row = sums[(at - 3) * ROWS : (at - 2) * ROWS, :INNER].astype(BF16).astype(F32)
            total = total + row * taps[k : k + 1, :]
        activ[n * ROWS : (n + 1) * ROWS, :] = silu(total).astype(BF16).astype(F32)
    act = activ[...].astype(BF16)
    low = dot(act, w_low[...]).reshape(2, BROWS // 2, RANK)
    sel = lax.dot_general(
        act, w_select[...], (((1,), (1,)), ((), ())), preferred_element_type=F32
    ).reshape(2, BROWS // 2, 128)
    pair_s[:, :, :RANK] = low
    pair_s[:, :, RANK:] = sel
    swap = rcopy(pair_s, pair_r, ss.at[0], rs.at[0], core)
    swap.start()
    swap.wait_recv()
    chip = pair_s[c] + pair_r[c]
    quad_s[...] = chip.astype(BF16)
    copies = [rcopy(quad_s, quad_r.at[n], ss.at[1 + n], rs.at[1 + n], others[n]) for n in range(3)]
    for copy in copies:
        copy.start()
    acc = quad_s[...].astype(F32)
    for n in range(3):
        copies[n].wait_recv()
        acc = acc + quad_r[n].astype(F32)
    full[c] = acc
    back = rcopy(full.at[c], full.at[c], ss.at[4], rs.at[4], core)
    back.start()
    rcopy(full.at[1 - c], full.at[1 - c], ss.at[4], rs.at[4], core).wait_recv()
    low_rank = full[:, :, :RANK].reshape(BROWS, RANK).astype(BF16)
    select[...] = full[:, :, RANK:].reshape(BROWS, 128)
    v = dot(low_rank, w_dt[...]) + dt_bias[...]
    step[...] = jnp.maximum(v, 0.0) + jnp.log1p(jnp.exp(-jnp.abs(v)))
    swap.wait_send()
    for copy in copies:
        copy.wait_send()
    back.wait_send()


def state_kernel(
    index, codes, scales, step, activ, select, sums, conv, decay_log, skip,
    gated, final, packed, source, new_codes, output, scale_rows, rates,
):
    lane = lax.broadcasted_iota(jnp.int32, (STATE, 128), 1)
    row_of = lax.broadcasted_iota(jnp.int32, (STATE, 128), 0)
    page_lane = lax.broadcasted_iota(jnp.int32, (1, 128), 1)
    width = 4 * PAGE

    def request(i, carry):
        b_in, c_out = [], []
        for n in range(STEPS):
            row = select[pl.ds(n * ROWS + i, 1), :]
            b_in.append(jnp.sum(jnp.where(lane == row_of, row, 0.0), axis=1, keepdims=True))
            c_out.append(
                jnp.sum(jnp.where(lane == row_of + STATE, row, 0.0), axis=1, keepdims=True)
            )
        kept = [jnp.zeros((1, 128), F32) for _ in range(STEPS)]
        for part in range(INNER // width):
            cols = slice(part * width, (part + 1) * width)
            rate = rates[:, cols]
            current = codes[i, :, cols].astype(F32) * scales[pl.ds(i, 1), cols]
            for n in range(STEPS):
                at = n * ROWS + i
                dt = step[pl.ds(at, 1), cols]
                act = activ[pl.ds(at, 1), cols]
                current = jnp.exp2(dt * rate) * current + (dt * act) * b_in[n]
                output[pl.ds(at, 1), cols] = jnp.sum(current * c_out[n], axis=0, keepdims=True)
                peak = jnp.max(jnp.abs(current), axis=0, keepdims=True)
                for page in range(4):
                    here = slice(page * PAGE, (page + 1) * PAGE)
                    top = jnp.max(peak[:, here], axis=1, keepdims=True)
                    scale = (top + 1e-06).astype(BF16).astype(F32)
                    kept[n] = jnp.where(page_lane == part * 4 + page, scale, kept[n])
                    new_codes[at, :, part * width + page * PAGE : part * width + (page + 1) * PAGE] = (
                        current[:, here] * (1.0 / scale)
                    ).astype(BF16)
        for n in range(STEPS):
            scale_rows[pl.ds(n * ROWS + i, 1), :] = kept[n]
        final[i] = new_codes[(STEPS - 1) * ROWS + i]
        return carry

    rates[...] = -jnp.exp(decay_log[...]) * 1.4426950408889634
    lax.fori_loop(0, ROWS, request, 0)
    gated[...] = (
        (output[...] + skip[...] * activ[...]) * silu(sums[:, INNER:])
    ).astype(BF16)
    for k in range(3):
        if k < 2:
            source[k * BROWS : (k + 1) * BROWS, :] = jnp.concatenate(
                [conv[(k + 1) * ROWS :, :], sums[: (k + 2) * ROWS, :INNER]], axis=0
            ).astype(BF16)
        else:
            source[k * BROWS : (k + 1) * BROWS, :] = sums[:, :INNER].astype(BF16)
    source[3 * BROWS :, :] = jnp.zeros((BROWS, INNER), BF16)
    source[3 * BROWS :, :128] = scale_rows[...].astype(BF16)

    def pack(n, carry):
        packed[n] = new_codes[index[n]]
        return carry

    lax.fori_loop(0, BLOCKS * PAIRS, pack, 0)


SIDE = 4 * PAIRS

BACK_SCRATCH = [
    pltpu.VMEM((BLOCKS, BROWS, INNER // 2), BF16),
    pltpu.VMEM((BLOCKS, BROWS, INNER // 2), BF16),
    pltpu.VMEM((BLOCKS, BROWS, FEATS), F32),
    pltpu.VMEM((BLOCKS, BROWS, FEATS), F32),
    pltpu.VMEM((BLOCKS, SIDE, INNER), BF16),
    pltpu.SemaphoreType.DMA((2, 16)),
    pltpu.SemaphoreType.DMA((2, 16)),
    pltpu.SemaphoreType.DMA((2, 16)),
    pltpu.SemaphoreType.DMA((2, 16)),
]


class Gather:
    def __init__(self, axis, buf, ss, rs):
        self.axes = (axis, 1 - axis)
        self.buf, self.ss, self.rs = buf, ss, rs
        self.q, self.p = req_place(axis), req_place(1 - axis)
        self.order = [self.q, mod4(self.q - 1), mod4(self.q + 1), mod4(self.q + 2)]
        self.sent = []

    def send(self, ref, n, axis, d):
        copy = rcopy(ref, ref, self.ss.at[n], self.rs.at[n], shift_req(axis, d))
        copy.start()
        self.sent.append(copy)

    def arrived(self, ref, n):
        rcopy(ref, ref, self.ss.at[n], self.rs.at[n], shift_req(self.axes[0], 1)).wait_recv()

    def block(self, p, q):
        return self.buf.at[p * 4 + q]

    def rows(self, p, q, h):
        return self.buf.at[p * 4 + q, pl.ds(h * (BROWS // 2), BROWS // 2)]

    def start(self):
        mine = self.block(self.p, self.q)
        self.send(mine, 0, self.axes[0], 1)
        self.send(mine, 1, self.axes[0], -1)
        self.spread(0)

    def spread(self, k):
        block = self.block(self.p, self.order[k])
        self.send(block, 4 + k, self.axes[1], 1)
        self.send(block, 8 + k, self.axes[1], -1)

    def near(self):
        self.arrived(self.block(self.p, self.order[1]), 0)
        self.send(self.rows(self.p, self.order[1], 0), 2, self.axes[0], 1)
        self.spread(1)
        self.arrived(self.block(self.p, self.order[2]), 1)
        self.send(self.rows(self.p, self.order[2], 1), 3, self.axes[0], -1)
        self.spread(2)

    def last(self):
        self.arrived(self.rows(self.p, self.order[3], 0), 2)
        self.arrived(self.rows(self.p, self.order[3], 1), 3)
        self.spread(3)

    def relay(self, k):
        below, above = mod4(self.p - 1), mod4(self.p + 1)
        self.arrived(self.block(below, self.order[k]), 4 + k)
        if k < 2:
            self.send(self.block(below, self.order[k]), 12 + k, self.axes[1], 1)
        self.arrived(self.block(above, self.order[k]), 8 + k)
        if k >= 2:
            self.send(self.block(above, self.order[k]), 12 + k, self.axes[1], -1)

    def end(self, k):
        self.arrived(self.block(mod4(self.p + 2), self.order[k]), 12 + k)

    def drain(self):
        for copy in self.sent:
            copy.wait_send()


def back_kernel(gated, w_out, want, source, packed, mixed, got_codes, got_side, *scratch):
    tp_bufs, rest = scratch[: len(TP_SCRATCH)], scratch[len(TP_SCRATCH) :]
    buf_a, buf_b, acc_a, acc_b, side, gss, grs, css, crs = rest
    r, t = lax.axis_index("req"), lax.axis_index("tp")
    x, z = lax.div(r, 4), lax.rem(r, 4)
    offsets = [(dx, dz) for dx in range(4) for dz in range(4) if (dx, dz) != (0, 0)]
    peers = [mod4(x + dx) * 4 + mod4(z + dz) for dx, dz in offsets]
    froms = [mod4(x - dx) * 4 + mod4(z - dz) for dx, dz in offsets]
    greet(tp_partners() + [(peer, t) for peer in peers])
    half = INNER // 2
    buf_a[r] = gated[:, :half]
    buf_b[z * 4 + x] = gated[:, half:]
    parts = [
        Gather(1, buf_a, gss.at[0], grs.at[0]),
        Gather(0, buf_b, gss.at[1], grs.at[1]),
    ]
    for part in parts:
        part.start()

    def project(part, p, k):
        buf, acc, rows = ((buf_a, acc_a, slice(0, half)), (buf_b, acc_b, slice(half, INNER)))[part]
        at = p * 4 + parts[part].order[k]
        acc[at] = dot(buf[at], w_out[rows, :])

    for n in range(4):
        rows = slice(n * 128, (n + 1) * 128)
        lane = lax.broadcasted_iota(jnp.int32, (128, 4 * BROWS), 1)
        hot = jnp.where(lane == want[rows, :], 1.0, 0.0).astype(BF16)
        side[4 * n : 4 * (n + 1)] = dot(hot, source[...]).astype(BF16).reshape(4, SIDE, INNER)
    for n in range(2):
        project(n, parts[n].p, 0)
    for part in parts:
        part.near()
    for n in range(2):
        project(n, parts[n].p, 1)
        project(n, parts[n].p, 2)
    for part in parts:
        part.last()
    for n in range(2):
        project(n, parts[n].p, 3)
    for k in range(4):
        for part in parts:
            part.relay(k)
        for n in range(2):
            project(n, mod4(parts[n].p - 1), k)
            project(n, mod4(parts[n].p + 1), k)
    saves = []
    for n, peer in enumerate(peers):
        saves.append(rcopy(packed.at[peer], got_codes.at[r], css.at[0, n], crs.at[0, n], (peer, t)))
        saves.append(rcopy(side.at[peer], got_side.at[r], css.at[1, n], crs.at[1, n], (peer, t)))
    for copy in saves:
        copy.start()
    local = [
        pltpu.make_async_copy(packed.at[r], got_codes.at[r], css.at[0, 15]),
        pltpu.make_async_copy(side.at[r], got_side.at[r], css.at[1, 15]),
    ]
    for copy in local:
        copy.start()
    for k in range(4):
        for n in range(2):
            parts[n].end(k)
            project(n, mod4(parts[n].p + 2), k)

    def summed(ch):
        both = []
        for h in range(2):
            b = 2 * ch + h
            both.append(acc_a[b] + acc_b[lax.rem(b, 4) * 4 + lax.div(b, 4)])
        return jnp.stack(both)

    tp_sum(summed, mixed, tp_bufs)
    for part in parts:
        part.drain()
    for n, src in enumerate(froms):
        rcopy(got_codes.at[src], got_codes.at[src], css.at[0, n], crs.at[0, n], (src, t)).wait_recv()
        rcopy(got_side.at[src], got_side.at[src], css.at[1, n], crs.at[1, n], (src, t)).wait_recv()
    for copy in saves:
        copy.wait_send()
    for copy in local:
        copy.wait()


def place_kernel(where_s, where_v, side, codes, out, win0, win1, win2, scale, zero, sems):
    zero[...] = jnp.zeros_like(zero)

    def begin(s, carry):
        at = where_s[s]

        @pl.when(at >= 0)
        def _():
            pltpu.make_async_copy(codes.at[at], out.at[s], sems.at[s]).start()

        @pl.when(at < 0)
        def _():
            pltpu.make_async_copy(zero, out.at[s], sems.at[s]).start()

        return carry

    lax.fori_loop(0, SLOTS, begin, 0)
    at = where_v[...]
    lane = lax.broadcasted_iota(jnp.int32, (SLOTS, BLOCKS * SIDE), 1)
    first = lax.div(at, PAIRS) * SIDE + lax.rem(at, PAIRS)
    for k, ref in enumerate((win0, win1, win2)):
        hot = jnp.where((lane == first + k * PAIRS) & (at >= 0), 1.0, 0.0).astype(BF16)
        ref[...] = dot(hot, side[...]).astype(BF16)
    hot = jnp.where((lane == first + 3 * PAIRS) & (at >= 0), 1.0, 0.0).astype(BF16)
    scale[...] = dot(hot, side[:, :128]).astype(BF16)

    def end(s, carry):
        pltpu.make_async_copy(zero, out.at[s], sems.at[s]).wait()
        return carry

    lax.fori_loop(0, SLOTS, end, 0)


def save_plan(finish, holder, slot_index, me):
    fin = finish.reshape(STEPS, BLOCKS, ROWS) == 1
    own = holder.reshape(STEPS, BLOCKS, ROWS)
    slot = slot_index.reshape(STEPS, BLOCKS, ROWS)
    earlier = jnp.arange(ROWS)[None, :] < jnp.arange(ROWS)[:, None]
    ahead = earlier & (own[..., None, :] == own[..., :, None]) & fin[..., None, :]
    ranks = jnp.sum(ahead.astype(jnp.int32), axis=3)
    block = lax.broadcasted_iota(jnp.int32, (STEPS, BLOCKS, ROWS), 1)
    step = lax.broadcasted_iota(jnp.int32, (STEPS, BLOCKS, ROWS), 0)
    value = block * PAIRS + step * CAP + ranks + 1
    taken = (fin & (own == me)).reshape(1, -1) & (
        slot.reshape(1, -1) == jnp.arange(SLOTS)[:, None]
    )
    where = jnp.sum(jnp.where(taken, value.reshape(1, -1), 0), axis=1) - 1
    fin_own = lax.dynamic_index_in_dim(fin, me, 1, False)
    own_own = lax.dynamic_index_in_dim(own, me, 1, False)
    rank_own = lax.dynamic_index_in_dim(ranks, me, 1, False)
    row = lax.broadcasted_iota(jnp.int32, (STEPS, ROWS), 0) * ROWS + lax.broadcasted_iota(
        jnp.int32, (STEPS, ROWS), 1
    )
    match = (
        fin_own[None, :, None, :]
        & (own_own[None, :, None, :] == jnp.arange(BLOCKS)[:, None, None, None])
        & (rank_own[None, :, None, :] == jnp.arange(CAP)[None, None, :, None])
    )
    index = jnp.sum(jnp.where(match, row[None, :, None, :] + 1, 0), axis=3).reshape(-1) - 1
    return index, where


def per_device(
    tokens, finish, holder, slot_index, embedding, norm_gain, proj_inner, proj_gate, conv_weight,
    conv_bias, proj_low, proj_select, proj_dt, dt_bias, decay_log, skip_gain, proj_out, state_codes,
    state_scales, conv_state,
):
    me = lax.axis_index("req")
    ids = tokens.reshape(STEPS, BLOCKS, ROWS).transpose(1, 0, 2).reshape(BLOCKS, BROWS, 1)
    ids = ids - lax.axis_index("tp") * embedding.shape[0]
    index, where = save_plan(finish, holder, slot_index, me)
    conv = conv_state.transpose(1, 0, 2).reshape(3 * ROWS, INNER).astype(F32)
    scales = jnp.repeat(state_scales.astype(F32), PAGE, axis=1)
    shape = jax.ShapeDtypeStruct
    sums = vmem_call(
        front_kernel, shape((BROWS, 2 * INNER), F32), 5, TP_SCRATCH + list(FRONT_SCRATCH),
        collective_id=0, has_side_effects=True,
    )(ids, embedding, norm_gain.reshape(1, -1), proj_inner, proj_gate)
    half = BROWS // 2
    select_pad = jnp.pad(proj_select, ((0, 128 - 2 * STATE), (0, 0)))
    step, activ, select = vmem_call(
        rank_kernel,
        [shape((BROWS, INNER), F32), shape((BROWS, INNER), F32), shape((BROWS, 128), F32)],
        8,
        [
            pltpu.VMEM((2, half, RCOLS), F32),
            pltpu.VMEM((2, half, RCOLS), F32),
            pltpu.VMEM((half, RCOLS), BF16),
            pltpu.VMEM((3, half, RCOLS), BF16),
            pltpu.VMEM((2, half, RCOLS), F32),
            pltpu.SemaphoreType.DMA((5,)),
            pltpu.SemaphoreType.DMA((5,)),
        ],
        collective_id=1, has_side_effects=True,
    )(
        sums, conv, conv_weight, conv_bias.reshape(1, -1), proj_low, select_pad, proj_dt,
        dt_bias.reshape(1, -1),
    )
    vmem = pl.BlockSpec(memory_space=pltpu.VMEM)
    smem = pl.BlockSpec(memory_space=pltpu.SMEM)
    anywhere = pl.BlockSpec(memory_space=pl.ANY)
    params = pltpu.CompilerParams(vmem_limit_bytes=VMEM_LIMIT)
    gated, final, packed, source = pl.pallas_call(
        state_kernel,
        out_shape=[
            shape((BROWS, INNER), BF16),
            shape((ROWS, STATE, INNER), BF16),
            shape((BLOCKS * PAIRS, STATE, INNER), BF16),
            shape((4 * BROWS, INNER), BF16),
        ],
        in_specs=[smem] + [vmem] * 9,
        out_specs=[vmem] * 4,
        scratch_shapes=[
            pltpu.VMEM((BROWS, STATE, INNER), BF16),
            pltpu.VMEM((BROWS, INNER), F32),
            pltpu.VMEM((BROWS, 128), F32),
            pltpu.VMEM((STATE, INNER), F32),
        ],
        compiler_params=params,
    )(
        jnp.maximum(index, 0), state_codes, scales, step, activ, select, sums, conv, decay_log,
        skip_gain.reshape(1, -1),
    )
    kind = jnp.arange(4, dtype=jnp.int32)[None, :, None] * BROWS
    want = index.reshape(BLOCKS, 1, PAIRS)
    want = jnp.where(want >= 0, want + kind, -1).reshape(BLOCKS * SIDE, 1)
    mixed, got_codes, got_side = pl.pallas_call(
        back_kernel,
        out_shape=[
            shape((BLOCKS, BROWS, FEATS), BF16),
            shape((BLOCKS, PAIRS, STATE, INNER), BF16),
            shape((BLOCKS, SIDE, INNER), BF16),
        ],
        in_specs=[vmem] * 4 + [anywhere],
        out_specs=[vmem, anywhere, anywhere],
        scratch_shapes=TP_SCRATCH + BACK_SCRATCH,
        compiler_params=pltpu.CompilerParams(
            vmem_limit_bytes=VMEM_LIMIT, collective_id=2, has_side_effects=True
        ),
    )(gated, proj_out, want, source, packed.reshape(BLOCKS, PAIRS, STATE, INNER))
    cache_codes, win0, win1, win2, cache_scales = pl.pallas_call(
        place_kernel,
        out_shape=[shape((SLOTS, STATE, INNER), BF16)]
        + [shape((SLOTS, INNER), BF16)] * 3
        + [shape((SLOTS, 128), BF16)],
        in_specs=[smem, vmem, vmem, anywhere],
        out_specs=[anywhere] + [vmem] * 4,
        scratch_shapes=[pltpu.VMEM((STATE, INNER), BF16), pltpu.SemaphoreType.DMA((SLOTS,))],
        compiler_params=params,
    )(
        where, where.reshape(-1, 1), got_side.reshape(BLOCKS * SIDE, INNER),
        got_codes.reshape(BLOCKS * PAIRS, STATE, INNER),
    )
    mixed = mixed.reshape(BLOCKS, STEPS, ROWS, FEATS).transpose(1, 0, 2, 3)
    mixed = mixed.reshape(STEPS, BLOCKS * ROWS, FEATS)
    last = slice((STEPS - 1) * ROWS, BROWS)
    pages = INNER // PAGE
    next_scales = source[3 * BROWS :][last, :pages]
    next_window = jnp.stack([source[k * BROWS : (k + 1) * BROWS][last] for k in range(3)], axis=1)
    cache_window = jnp.stack([win0, win1, win2], axis=1)
    return (
        mixed, final, next_scales, next_window, cache_codes, cache_scales[:, :pages], cache_window,
    )


def solution(mesh):
    in_specs = (
        P(), P(), P(), P(), P("tp", "req"), P("req"), P("req", "tp"), P("req", "tp"),
        P(None, "tp"), P("tp"), P("tp", None), P(None, "tp"), P(None, "tp"), P("tp"),
        P(None, "tp"), P("tp"), P("tp", "req"), P("req", None, "tp"), P("req", "tp"),
        P("req", None, "tp"),
    )
    out_specs = (
        P(None, None, "req"), P("req", None, "tp"), P("req", "tp"), P("req", None, "tp"),
        P("req", None, "tp"), P("req", "tp"), P("req", None, "tp"),
    )
    return jax.shard_map(
        per_device, mesh=mesh, in_specs=in_specs, out_specs=out_specs, check_vma=False
    )
```

time: 817 us -> 520 us (0.64); the launches traced: 806 us -> 520 us
  Pallas kernels: 0 us -> 499 us
  waiting for transfers between devices: 425 us -> 0 us
  local copies, waits for them, and re-layouts: 121 us -> 11.6 us
  matrix products: 77.4 us -> 0 us
  starting transfers between devices: 70.1 us -> 0 us
  other arithmetic: 62.5 us -> 7.82 us
  blocking collectives: 33.8 us -> 0 us
  between operations: 16.6 us -> 0.83 us
    pallas_call x0 -> x5, Pallas kernels: none -> 499 us  [the longest x1 221 us: per_device(): pl.pallas_call(back_kernel, out_shape=[shape((BLOCKS, BROWS, FEATS), BF16...]
    psum x3 -> x0, waiting for transfers between devices: 178 us -> none  [the longest x1 61.6 us: per_device(): mixed_steps.append(lax.psum(projected.astype(jnp.bfloat16), 'tp'))]
    unnamed x9 -> x0, waiting for transfers between devices: 174 us -> none
    dot_general x48 -> x0, matrix products: 77.4 us -> none  [the longest x4 22.8 us: per_device(): jnp.dot(normed, joined, preferred_element_type=jnp.float32)]
    all_to_all x12 -> x0, starting transfers between devices: 69.4 us -> none  [the longest x4 29.4 us: per_device(): lax.all_to_all(send_codes, 'req', split_axis=0, concat_axis=0, tiled=True)]
    unnamed x211 -> x14, local copies, waits for them, and re-layouts: 66 us -> 2.82 us
    all_to_all x12 -> x0, waiting for transfers between devices: 58.5 us -> none  [the longest x4 36.5 us: per_device(): lax.all_to_all(send_codes, 'req', split_axis=0, concat_axis=0, tiled=True)]
    psum x1 -> x0, blocking collectives: 33.8 us -> none  [per_device(): squares = lax.psum(jnp.sum(embedded * embedded, axis=2), 'req')]
  transfers between devices with their start and end apart: 20 -> 0, of which waited for: 15 -> 0; matrix products, arithmetic and copies ran while one was open for 20% -> 0% of each run, Pallas kernels for 0% -> 0%
where the time goes in v1:
time: 520 us
  Pallas kernels  499 us (96%)
  local copies, waits for them, and re-layouts  11.6 us (2%)
  other arithmetic  7.82 us (2%)
    pallas_call x1, Pallas kernels, per_device(): pl.pallas_call(back_kernel, out_shape=[shape((BLOCKS, BROWS, FEATS), BF16...  221 us
    pallas_call x1, Pallas kernels, per_device(): pl.pallas_call(place_kernel, out_shape=[shape((SLOTS, STATE, INNER), BF16...  131 us
    pallas_call x1, Pallas kernels, per_device(): vmem_call(front_kernel, shape((BROWS, 2 * INNER), F32), 5, TP_SCRATCH + l...  110 us
    pallas_call x1, Pallas kernels, per_device(): pl.pallas_call(state_kernel, out_shape=[shape((BROWS, INNER), BF16), shap...  19.4 us
    pallas_call x1, Pallas kernels, per_device(): vmem_call(rank_kernel, [shape((BROWS, INNER), F32), shape((BROWS, INNER),...  17.3 us

profile of v1, /device:TPU:1, one launch (start us, length us, event | category | flops | bytes accessed | tf_op | source)
XLA Modules:
  0.0 519.6 jit_solution(1820225936925775845)
XLA Ops:
  0.6 0.7 compare_and_fusion
  1.4 0.1 eq.95
  1.5 0.8 reshape.243
  2.3 1.4 convert_reduce_fusion
  3.8 0.1 add_add_fusion.1
  3.8 0.2 select_reduce_fusion.1
  4.1 0.1 copy.58
  4.1 0.1 copy.57
  4.2 0.1 add_select_fusion
  4.3 0.8 select_n.34.want
  5.2 0.1 copy.53
  5.3 0.7 max.10.index
  5.9 0.7 broadcast_subtract_fusion
  6.6 0.1 sub.27
  6.7 1.2 sub.33.ids
  7.9 0.0 copy-start.1
  7.9 0.0 copy-start.2
  7.9 110.3 %shard_map.243.sums = f32[96,4096]{1,0:T(8,128)} custom-call(s32[16,96,1]{2,1,0:T(8,128)} %sub.33.ids, bf16[4096,512]{1,0:T(8,128)(2,1)} %emb.1, f32[1,512]{1,0:T(1,128)} %bitcast.62, bf16[512,2048]{1,0:T(8,128)(2,1)} %w_inner.1, bf16[512,2048]{1,0:T(8,128)(2,1)} %w_gate.1), custom_call_target="tpu_custom_call" | custom-call | tf_op jit(solution)/shard_map/pallas_call | solution.py:702
  118.2 0.0 copy-done.1
  118.2 0.9 convert_element_type.21
  119.1 0.0 copy-done.2
  119.1 0.8 pad.4.w_select
  119.9 0.0 copy-start.4
  119.9 17.3 %shard_map.244 = (f32[96,2048]{1,0:T(8,128)}, f32[96,2048]{1,0:T(8,128)}, f32[96,128]{1,0:T(8,128)}) custom-call(f32[96,4096]{1,0:T(8,128)} %shard_map.243.sums, f32[72,2048]{1,0:T(8,128)} %bitcast.43, f32[4,2048]{1,0:T(4,128)} %taps.1, f32[1,2048]{1,0:T(1,128)} %bitcast.57, bf16[2048,512]{1,0:T(8,128)(2,1)} %w_low.1, bf16[128,2048]{1,0:T(8,128)(2,1)} %pad.4.w_select, ...), custom_call_target="tpu_custom_call" | custom-call | tf_op jit(solution)/shard_map/pallas_call | solution.py:708
  137.3 0.0 copy-done.4
  137.3 0.1 copy.54
  137.3 0.1 broadcast_in_dim.53
  137.5 0.7 copy.70
  138.2 19.4 %shard_map.245 = (bf16[96,2048]{1,0:T(8,128)(2,1)}, bf16[24,16,2048]{2,1,0:T(8,128)(2,1)}, bf16[128,16,2048]{2,1,0:T(8,128)(2,1)}, bf16[384,2048]{1,0:T(8,128)(2,1)}) custom-call(s32[128]{0:T(128)} %max.10.index, bf16[24,16,2048]{2,1,0:T(8,128)(2,1)} %codes.1, f32[24,2048]{1,0:T(8,128)} %bitcast.48, f32[96,2048]{1,0:T(8,128)} %get-tuple-element.22.step, ...), custom_call_target="tpu_custom_call" | custom-call | tf_op jit(solution)/shard_map/pallas_call | solution.py:730
  157.6 0.0 copy-start.3
  157.6 221.1 %shard_map.246 = (bf16[16,96,512]{2,1,0:T(8,128)(2,1)}, bf16[16,8,16,2048]{3,2,1,0:T(8,128)(2,1)}, bf16[16,32,2048]{2,1,0:T(8,128)(2,1)}) custom-call(bf16[96,2048]{1,0:T(8,128)(2,1)} %get-tuple-element.25.gated, bf16[2048,512]{1,0:T(8,128)(2,1)} %w_out.1, s32[512,1]{1,0:T(8,128)} %select_n.34.want, bf16[384,2048]{1,0:T(8,128)(2,1)} %get-tuple-element.26.source, ...), custom_call_target="tpu_custom_call" | custom-call | tf_op jit(solution)/shard_map/pallas_call | solution.py:754
  378.7 0.1 add_add_fusion
  378.8 0.1 add.104
  378.9 0.0 copy-done.3
  378.9 0.2 select_reduce_fusion
  379.1 0.5 fusion.2
  379.6 0.7 copy.61.where_v
  380.3 131.2 %shard_map.247 = (bf16[64,16,2048]{2,1,0:T(8,128)(2,1)}, bf16[64,2048]{1,0:T(8,128)(2,1)}, bf16[64,2048]{1,0:T(8,128)(2,1)}, bf16[64,2048]{1,0:T(8,128)(2,1)}, bf16[64,128]{1,0:T(8,128)(2,1)}) custom-call(s32[64]{0:T(128)} %get-tuple-element.66.where_s, s32[64,1]{1,0:T(8,128)} %copy.61.where_v, bf16[512,2048]{1,0:T(8,128)(2,1)} %bitcast.45, ...), custom_call_target="tpu_custom_call" | custom-call | tf_op jit(solution)/shard_map/pallas_call | solution.py:768
  511.6 0.0 copy-start
  511.6 2.2 pad_maximum_fusion
  513.8 1.4 copy.63
  515.1 1.0 slice_bitcast_fusion.2
  516.1 0.7 pad_maximum_fusion.1
  516.9 0.0 copy-done
  516.9 1.3 copy.60
  518.2 0.7 slice.23
  518.9 0.7 copy.62
  (15 shorter events, 0.1 us)
Async XLA Ops:
  7.9 110.3 %copy-start.1 = (bf16[24,3,2048]{2,0,1:T(8,128)(2,1)S(1)}, bf16[24,3,2048]{2,0,1:T(8,128)(2,1)}, u32[]{:S(2)}) copy-start(bf16[24,3,2048]{2,0,1:T(8,128)(2,1)} %param.39) | copy-start | bytes 884740
  7.9 111.2 %copy-start.2 = (bf16[32,2048]{1,0:T(8,128)(2,1)S(1)}, bf16[32,2048]{1,0:T(8,128)(2,1)}, u32[]{:S(2)}) copy-start(bf16[32,2048]{1,0:T(8,128)(2,1)} %param.31) | copy-start | bytes 393220
  119.9 17.4 %copy-start.4 = (bf16[24,16]{0,1:T(8,128)(2,1)S(1)}, bf16[24,16]{0,1:T(8,128)(2,1)}, u32[]{:S(2)}) copy-start(bf16[24,16]{0,1:T(8,128)(2,1)} %param.38) | copy-start | bytes 2308
  157.6 221.3 %copy-start.3 = (s32[4,384]{1,0:T(4,128)S(1)}, s32[4,384]{1,0:T(4,128)}, u32[]{:S(2)}) copy-start(s32[4,384]{1,0:T(4,128)} %param.23) | copy-start | bytes 18436
  511.6 5.3 %copy-start = (bf16[16,96,512]{2,1,0:T(8,128)(2,1)S(1)}, bf16[16,96,512]{2,1,0:T(8,128)(2,1)}, u32[]{:S(2)}) copy-start(bf16[16,96,512]{2,1,0:T(8,128)(2,1)} %get-tuple-element.28) | copy-start | bytes 4718596
